TPU v7x, 128 devices: a whole 4x4x4 slice. The times are simulated.
128 devices in a mesh: shell: 8 (over x, z_hi), rank: 16 (over z_lo, y, core).
Axes of the slice: x: 4, y: 4, z: 4 (z_hi: 2, z_lo: 2; z = z_hi * 2 + z_lo), core: 2. Of those that a mesh axis runs over, the one named last changes fastest.
Arguments:
- coefs: float32 [16, 3, 65536], P(None, None, ('shell', 'rank')), may hold values from -3 to 3
- radii: float32 [65536], P(('shell', 'rank')), may hold values from 0.5 to 2
- pair_blocks: int32 [2, 1024], P(None, ('shell', 'rank')), may hold values from 0 to 63, as said below
- pair_count: int32 [128], P(('shell', 'rank')), may hold values from 1 to 8
Outputs:
- intensity: float32 [65536], P(('shell', 'rank'))
Inputs may be any that keep to these rules, and one draw needn't show every extreme that they name: pair_blocks[0] is below 32; pair_blocks[1] differs from pair_blocks[0] and is below 32 in slots of the last shell group.
All inputs are finite; a program needn't handle non-finite values.
Results may differ from a plain program's by a relative error of at most 0.0003.
Values sent between devices are 32-bit elements; how exact they have to be, the bound alone decides.
No kernel may reach another device: no remote copies, remote signals or barrier semaphores. Data moves between devices by JAX's collectives and lax.ppermute only.
A program may use at most 64 MiB of HBM per device.

v0:
```python
import jax
import jax.numpy as jnp
import numpy as np
from jax import lax
from jax.experimental import pallas as pl
from jax.experimental.pallas import tpu as pltpu
from jax.sharding import PartitionSpec as P

NCOEF = 16
TIMES = 64
BLOCK = 256
RANKS = 16
SLOTS = 8
BLOCKS = 32
SPAN = BLOCKS * BLOCK
HELD = 512
UNROLL = 8
LIST = 160
LISTS = 512
COUNTS = 480
TILE = 64
F32 = jnp.float32
BF16 = jnp.bfloat16
VMEM = pltpu.VMEM
SMEM = pltpu.SMEM
PARAMS = pltpu.CompilerParams(vmem_limit_bytes=24 * 1024 * 1024)


def passed_along(value, axis, steps):
    count = lax.axis_size(axis)
    leading, last = (max(0, -steps), min(count, count - steps))
    return lax.ppermute(value, axis, [(source, source + steps) for source in range(leading, last)])


EIGHT = ((0, 0), (0, 1), (0, 2), (3, 0), (1, 0), (1, 1), (1, 2), (3, 1))
FOUR = ((2, 0), (2, 1), (2, 2), (3, 2))
CHUNK = 56


def spread_table():
    node = -1.0 + (2.0 * np.arange(TIMES) + 1.0) / TIMES
    table = np.cos(np.arange(NCOEF)[None, :] * np.arccos(node)[:, None])
    spread = np.zeros((RANKS, 16, 3, NCOEF), np.float32)
    for row, (time, coordinate) in enumerate(EIGHT + FOUR + FOUR):
        spread[:, row, coordinate, :] = table[time :: TIMES // RANKS]
    return spread.reshape(RANKS * 16, 3 * NCOEF)


def evaluate_kernel(*refs):
    given, (out, *held, sems) = refs[:5], refs[5:]
    copies = [pltpu.make_async_copy(given[i], held[i], sems.at[i]) for i in range(5)]
    for copy in copies:
        copy.start()
    for copy in copies:
        copy.wait()
    pairs, count, table, coefs, radii = held
    values = jnp.dot(
        table[...], coefs[...].reshape(3 * NCOEF, HELD), precision=lax.Precision.HIGHEST, preferred_element_type=F32
    ).reshape(RANKS, 16, HELD)
    lane = lax.broadcasted_iota(jnp.int32, (1, 128), 1)
    row = lax.broadcasted_iota(jnp.int32, (8, 128), 0)
    last = jnp.where(row == 6, count[0].astype(F32), 0.0)
    for q in range(4):
        last = jnp.where(row == q, radii[128 * q : 128 * q + 128].reshape(1, 128), last)
    for side in range(2):
        blocks = jnp.zeros((1, 128), F32)
        for slot in range(SLOTS):
            blocks = jnp.where(lane == slot, pairs[side, slot].astype(F32), blocks)
        last = jnp.where(row == 4 + side, blocks, last)
    runs = [values[:, :, 128 * q : 128 * q + 128] for q in range(4)]
    for q in range(4):
        out[:, 8 * q : 8 * q + 8, :] = runs[q][:, 0:8]
    for half in range(2):
        out[:, 32 + 8 * half : 40 + 8 * half, :] = jnp.where(
            row[None] < 4, runs[2 * half][:, 8:16], runs[2 * half + 1][:, 8:16]
        )
    out[:, 48:56, :] = jnp.broadcast_to(last[None], (RANKS, 8, 128))


def list_pairs(received):
    first, second, count = (received[:, row, 0:128] for row in (52, 53, 54))
    lane = lax.broadcasted_iota(jnp.int32, (RANKS, 128), 1)
    live = (lane < SLOTS) & (lane.astype(F32) < count)
    before_lane = jnp.where(
        lax.broadcasted_iota(jnp.int32, (128, 128), 0) < lax.broadcasted_iota(jnp.int32, (128, 128), 1), 1.0, 0.0
    ).astype(BF16)
    before_rank = jnp.where(
        lax.broadcasted_iota(jnp.int32, (RANKS, RANKS), 1) < lax.broadcasted_iota(jnp.int32, (RANKS, RANKS), 0), 1.0, 0.0
    ).astype(BF16)
    ones = jnp.ones((128, 128), BF16)
    crosses = second >= BLOCKS
    place = jnp.full((RANKS, 128), -1.0, F32)
    totals = []
    for which, chosen in enumerate((live & ~crosses, live & crosses)):
        flag = jnp.where(chosen, 1.0, 0.0).astype(BF16)
        within = jnp.dot(flag, before_lane, preferred_element_type=F32)
        ranks = jnp.dot(before_rank, flag, preferred_element_type=F32).astype(BF16)
        position = within + jnp.dot(ranks, ones, preferred_element_type=F32)
        place = jnp.where(chosen, position + which * LIST, place)
        totals.append(jnp.sum(flag.astype(F32), keepdims=True))
    second = jnp.where(crosses, second - BLOCKS, second)
    target = lax.broadcasted_iota(jnp.int32, (RANKS, LISTS), 1).astype(F32)
    sides = [jnp.zeros((RANKS, LISTS), F32)] * 2
    for slot in range(SLOTS):
        hit = place[:, slot : slot + 1] == target
        sides = [
            kept + jnp.where(hit, side[:, slot : slot + 1] - BLOCKS, 0.0) for kept, side in zip(sides, (first, second))
        ]
    lists = jnp.concatenate([jnp.sum(side, axis=0, keepdims=True) for side in sides], axis=0) + BLOCKS
    for which, total in enumerate(totals):
        lists = jnp.where(target[0:2] == COUNTS + which, total, lists)
    return lists.astype(jnp.int32)


def pieces(x):
    high = x.astype(BF16)
    rest = x - high.astype(F32)
    mid = rest.astype(BF16)
    low = (rest - mid.astype(F32)).astype(BF16)
    return high, mid, low


def radii_of(received, rank):
    return jnp.concatenate([received[rank, 48 + q : 49 + q, :] for q in range(4)], axis=1)


def features(received, rank):
    n = HELD
    radii = radii_of(received, rank)
    row = lax.broadcasted_iota(jnp.int32, (8, n), 0)
    eight = jnp.concatenate([received[rank, 8 * q : 8 * q + 8, :] for q in range(4)], axis=1)
    four = []
    for half in range(2):
        both = received[rank, 32 + 8 * half : 40 + 8 * half, :]
        four += [both, pltpu.roll(both, 4, 0)]
    four = jnp.concatenate(four, axis=1)
    upper = jnp.where(row % 4 == 3, radii, eight)
    lower = jnp.where(row < 3, four, radii)
    for at, moved in ((4, pltpu.roll(eight, 1, 0)), (5, pltpu.roll(eight, 6, 0)), (6, pltpu.roll(four, 3, 0))):
        lower = jnp.where(row == at, moved, lower)
    part = lax.broadcasted_iota(jnp.int32, (16, n), 0) % 4
    values = jnp.concatenate([upper, lower], axis=0)
    square = (values * values).reshape(2, 8, n)
    row = lax.broadcasted_iota(jnp.int32, (2, 8, n), 1)
    twos = square + jnp.where(row % 2 == 1, pltpu.roll(square, 1, 1), pltpu.roll(square, 7, 1))
    fours = twos + jnp.where((row // 2) % 2 == 1, pltpu.roll(twos, 2, 1), pltpu.roll(twos, 6, 1))
    high, mid, low = pieces(values)
    s_high, s_mid, s_low = (p.astype(F32) for p in pieces(fours.reshape(16, n)))
    zero = jnp.zeros((16, n), F32)
    sums = jnp.where(part == 0, s_high, jnp.where(part == 1, s_mid, jnp.where(part == 2, s_low, zero)))
    ones = jnp.where(part == 3, zero, 1.0)
    return high, mid, low, sums, ones, part


def prepare_second(second, second_radii, received, rank):
    high, mid, low, sums, ones, _ = features(received, rank)
    radii = radii_of(received, rank)
    terms = (high, mid, high, low, high, mid, sums.astype(BF16), ones.astype(BF16))
    for i, term in enumerate(terms):
        second[16 * i : 16 * i + 16, rank * HELD : (rank + 1) * HELD] = term
    for half in range(HELD // BLOCK):
        block = rank * (HELD // BLOCK) + half
        second_radii[block : block + 1, :] = radii[:, half * BLOCK : (half + 1) * BLOCK]


def prepare_first(first, first_radii, received, rank):
    high, mid, low, sums, ones, part = features(received, rank)
    radii = radii_of(received, rank)
    scale = jnp.where(part == 3, 2.0, -2.0)
    high, mid, low = (scale * p.astype(F32) for p in (high, mid, low))
    terms = jnp.concatenate([high, high, mid, high, low, mid, ones, sums], axis=0)
    for c in range(0, HELD, 128):
        at = rank * HELD + c
        first[at : at + 128, :] = terms[:, c : c + 128].T.astype(BF16)
        first_radii[at : at + 128, :] = jnp.broadcast_to(radii[:, c : c + 128], (128, 128)).T


def credit_pair(first, first_radii, second, second_radii, rows, columns, a, b):
    from_a = pl.multiple_of(lax.rem(a, BLOCKS) * BLOCK, BLOCK)
    block_b = lax.rem(b, BLOCKS)
    of_b = second[:, pl.ds(pl.multiple_of(block_b * BLOCK, BLOCK), BLOCK)]
    radii_b = second_radii[pl.ds(block_b, 1), :]
    lane = lax.broadcasted_iota(jnp.int32, (TILE, 128), 1)
    masks = [jnp.where((lane % 16) // 4 == t, 1.0, 0.0).astype(BF16) for t in range(4)]
    column = jnp.zeros((8, BLOCK), F32)
    for i in range(0, BLOCK, TILE):
        of_a = first[pl.ds(from_a + i, TILE), :]
        total = None
        for mask in masks:
            whole = jnp.dot(of_a * mask, of_b, preferred_element_type=F32)
            inverse = pl.reciprocal(whole, approx=False)
            total = inverse if total is None else total + inverse
        radii_a = first_radii[pl.ds(from_a + i, TILE), :]
        summed = jnp.concatenate([radii_a, radii_a], axis=1) + radii_b
        weight = total * (summed * summed)
        column = column + jnp.sum(weight.reshape(TILE // 8, 8, BLOCK), axis=0)
        row = jnp.sum(weight[:, :128] + weight[:, 128:], axis=1, keepdims=True)
        rows[i : i + TILE, :] = rows[i : i + TILE, :] + jnp.where(lane == a, row, 0.0)
    at = pl.ds(pl.multiple_of(b * 8, 8), 8)
    columns[at, :] = columns[at, :] + column


def credit_list(first, first_radii, second, second_radii, rows, columns, lists, which):
    @pl.loop(0, (lists[0, COUNTS + which] + UNROLL - 1) // UNROLL)
    def _(step):
        for u in range(UNROLL):
            at = which * LIST + step * UNROLL + u
            credit_pair(first, first_radii, second, second_radii, rows, columns, lists[0, at], lists[1, at])


def block_sums(columns):
    return jnp.sum(columns[0 : 8 * BLOCKS, :].reshape(BLOCKS, 8, BLOCK), axis=1)


def own_kernel(
    received, rows, credited, first, first_radii, lists,
    second, second_radii, columns, listed, sem,
):
    lists[...] = list_pairs(received)
    copy = pltpu.make_async_copy(lists, listed, sem)
    copy.start()
    rows[...] = jnp.zeros_like(rows)
    columns[...] = jnp.zeros_like(columns)
    for rank in range(RANKS):
        prepare_second(second, second_radii, received, rank)
        prepare_first(first, first_radii, received, rank)
    copy.wait()
    credit_list(first, first_radii, second, second_radii, rows, columns, listed, 0)
    credited[...] = block_sums(columns)


def cross_kernel(
    lists, received, earlier_rows, earlier, first, first_radii, out,
    second, second_radii, rows, columns,
):
    rows[...] = earlier_rows[...]
    columns[...] = jnp.zeros_like(columns)
    for rank in range(RANKS):
        prepare_second(second, second_radii, received, rank)
    credit_list(first, first_radii, second, second_radii, rows, columns, lists, 1)
    factor = 1.0 / (TIMES * BLOCK)
    own = (earlier[...] + rows[...].T[0:BLOCKS, :]) * factor
    beyond = block_sums(columns) * factor
    for block in range(BLOCKS):
        rank, half = divmod(block, 2)
        for k in range(2):
            at = 2 * half + k
            out[rank, at : at + 1, :] = own[block : block + 1, k * 128 : (k + 1) * 128]
            out[rank, 4 + at : 5 + at, :] = beyond[block : block + 1, k * 128 : (k + 1) * 128]


def body(coefs, radii, pair_blocks, pair_count):
    in_vmem, in_smem = pl.BlockSpec(memory_space=VMEM), pl.BlockSpec(memory_space=SMEM)
    table = jnp.asarray(spread_table())
    coefs = coefs.transpose(1, 0, 2)
    at_all = pl.pallas_call(
        evaluate_kernel,
        out_shape=jax.ShapeDtypeStruct((RANKS, CHUNK, 128), F32),
        in_specs=[pl.BlockSpec(memory_space=pltpu.HBM)] * 5,
        out_specs=in_vmem,
        scratch_shapes=[
            SMEM(pair_blocks.shape, jnp.int32),
            SMEM(pair_count.shape, jnp.int32),
            VMEM(table.shape, F32),
            VMEM(coefs.shape, F32),
            VMEM(radii.shape, F32),
            pltpu.SemaphoreType.DMA((5,)),
        ],
        compiler_params=pltpu.CompilerParams(vmem_limit_bytes=60 * 1024 * 1024),
        name="evaluate",
    )(pair_blocks, pair_count, table, coefs, radii)
    received = lax.all_to_all(at_all, "rank", 0, 0)
    beyond = passed_along(received, "shell", -1)
    rows, credited, first, first_radii, lists = pl.pallas_call(
        own_kernel,
        out_shape=[
            jax.ShapeDtypeStruct((BLOCK, 128), F32),
            jax.ShapeDtypeStruct((BLOCKS, BLOCK), F32),
            jax.ShapeDtypeStruct((SPAN, 128), BF16),
            jax.ShapeDtypeStruct((SPAN, 128), F32),
            jax.ShapeDtypeStruct((2, LISTS), jnp.int32),
        ],
        in_specs=[in_vmem],
        out_specs=[in_vmem] * 5,
        scratch_shapes=[
            VMEM((128, SPAN), BF16),
            VMEM((BLOCKS, BLOCK), F32),
            VMEM((8 * BLOCKS + 8, BLOCK), F32),
            SMEM((2, LISTS), jnp.int32),
            pltpu.SemaphoreType.DMA,
        ],
        compiler_params=PARAMS,
        cost_estimate=pl.CostEstimate(flops=8_000_000_000, bytes_accessed=8_000_000, transcendentals=0),
        name="own_pairs",
    )(received)
    partial = pl.pallas_call(
        cross_kernel,
        out_shape=jax.ShapeDtypeStruct((RANKS, 8, 128), F32),
        in_specs=[in_smem] + [in_vmem] * 5,
        out_specs=in_vmem,
        scratch_shapes=[
            VMEM((128, SPAN), BF16),
            VMEM((BLOCKS, BLOCK), F32),
            VMEM((BLOCK, 128), F32),
            VMEM((8 * BLOCKS + 8, BLOCK), F32),
        ],
        compiler_params=PARAMS,
        cost_estimate=pl.CostEstimate(flops=8_000_000_000, bytes_accessed=8_000_000, transcendentals=0),
        name="crossing_pairs",
    )(lists, beyond, rows, credited, first, first_radii)
    summed = jnp.sum(lax.all_to_all(partial, "rank", 0, 0), axis=0)
    returned = passed_along(summed[4:], "shell", 1)
    return (summed[:4] + returned).reshape(HELD)


def solution(mesh):
    placed = (
        P(None, None, ("shell", "rank")),
        P(("shell", "rank")),
        P(None, ("shell", "rank")),
        P(("shell", "rank")),
    )
    return jax.shard_map(
        body, mesh=mesh, in_specs=placed, out_specs=P(("shell", "rank")), check_vma=False
    )
```

profile of v0, /device:TPU:4, one launch (start us, length us, event | category | flops | bytes accessed | tf_op | source)
XLA Modules:
  0.0 65.4 jit_solution(479002857112923403)
XLA Ops:
  0.7 2.3 %evaluate.1 = f32[16,56,128]{2,1,0:T(8,128)} custom-call(s32[2,8]{1,0:T(2,128)} %refs_0_.1, s32[1]{0:T(128)S(6)} %copy.6.refs_1_, f32[256,48]{1,0:T(8,128)} %constant.4.clone.refs_2_, f32[3,16,512]{2,1,0:T(8,128)} %bitcast.3, f32[512]{0:T(512)} %refs_4_.1), custom_call_target="tpu_custom_call" | custom-call | tf_op jit(solution)/shard_map/evaluate/pallas_call | solution.py:256
  3.0 16.1 %all_to_all.10.received = f32[16,56,128]{2,1,0:T(8,128)S(1)} all-to-all(f32[16,56,128]{2,1,0:T(8,128)} %evaluate.1), channel_id=1, replica_groups=mesh['shell'=8,'rank'=16] {'rank'}, dimensions={0} | all-to-all | bytes 917504 | tf_op jit(solution)/shard_map/all_to_all | solution.py:272
  19.1 5.4 %collective-permute-start = (f32[16,56,128]{2,1,0:T(8,128)S(1)}, f32[16,56,128]{2,1,0:T(8,128)S(1)}, u32[]{:S(2)}, u32[]{:S(2)}) collective-permute-start(f32[16,56,128]{2,1,0:T(8,128)S(1)} %all_to_all.10.received), channel_id=1, source_target_pairs={{16,0},{32,16},{48,32},{64,48},{80,64},{96,80},{112,96},{17,1},{33... | collective-permute-start | bytes 1376264 | tf_op jit(solution)/shard_map/ppermute | solution.py:32
  24.5 12.6 %own_pairs.1 = (f32[256,128]{1,0:T(8,128)S(1)}, f32[32,256]{1,0:T(8,128)S(1)}, bf16[8192,128]{1,0:T(8,128)(2,1)S(1)}, f32[8192,128]{1,0:T(8,128)S(1)}, s32[2,512]{1,0:T(2,128)S(1)}) custom-call(f32[16,56,128]{2,1,0:T(8,128)S(1)} %all_to_all.10.received), custom_call_target="tpu_custom_call" | custom-call | flops 8000000000 | bytes 8000000 | tf_op jit(solution)/shard_map/own_pairs/pallas_call | solution.py:274
  37.1 0.0 collective-permute-done.received
  37.1 11.0 %crossing_pairs.1 = f32[16,8,128]{2,1,0:T(8,128)S(1)} custom-call(s32[2,512]{1,0:T(2,128)S(1)} %get-tuple-element.10.lists, f32[16,56,128]{2,1,0:T(8,128)S(1)} %collective-permute-done.received, f32[256,128]{1,0:T(8,128)S(1)} %get-tuple-element.11.earlier_rows, f32[32,256]{1,0:T(8,128)S(1)} %get-tuple-element.12.earlier, ...), custom_call_target="tpu_custom_call" | custom-call | flops 8000000000 | bytes 8000000 | tf_op jit(solution)/shard_map/crossing_pairs/pallas_call | solution.py:296
  48.2 8.7 %all_to_all.11 = f32[16,8,128]{2,1,0:T(8,128)S(1)} all-to-all(f32[16,8,128]{2,1,0:T(8,128)S(1)} %crossing_pairs.1), channel_id=1, replica_groups=mesh['shell'=8,'rank'=16] {'rank'}, dimensions={0} | all-to-all | bytes 131072 | tf_op jit(solution)/shard_map/all_to_all | solution.py:311
  56.9 1.9 %collective-permute-start.1 = (f32[4,128]{1,0:T(4,128)S(1)}, f32[4,128]{1,0:T(4,128)S(1)}, u32[]{:S(2)}, u32[]{:S(2)}) collective-permute-start(f32[4,128]{1,0:T(4,128)S(1)} %slice.7), channel_id=1, source_target_pairs={{0,16},{16,32},{32,48},{48,64},{64,80},{80,96},{96,112},{1,17},{17... | collective-permute-start | bytes 6152 | tf_op jit(solution)/shard_map/ppermute | solution.py:32
  58.8 6.0 %collective-permute-done.1 = f32[4,128]{1,0:T(4,128)S(1)} collective-permute-done((f32[4,128]{1,0:T(4,128)S(1)}, f32[4,128]{1,0:T(4,128)S(1)}, u32[]{:S(2)}, u32[]{:S(2)}) %collective-permute-start.1) | collective-permute-done | bytes 2080 | tf_op jit(solution)/shard_map/ppermute | solution.py:32
  64.8 0.6 add_bitcast_fusion
  (2 shorter events, 0.0 us)
Async XLA Ops:
  19.1 18.0 %collective-permute-start = (f32[16,56,128]{2,1,0:T(8,128)S(1)}, f32[16,56,128]{2,1,0:T(8,128)S(1)}, u32[]{:S(2)}, u32[]{:S(2)}) collective-permute-start(f32[16,56,128]{2,1,0:T(8,128)S(1)} %all_to_all.10.received), channel_id=1, source_target_pairs={{16,0},{32,16},{48,32},{64,48},{80,64},{96,80},{112,96},{17,1},{33... | collective-permute-start | bytes 1376264 | tf_op jit(solution)/shard_map/ppermute | solution.py:32
  56.9 7.9 %collective-permute-start.1 = (f32[4,128]{1,0:T(4,128)S(1)}, f32[4,128]{1,0:T(4,128)S(1)}, u32[]{:S(2)}, u32[]{:S(2)}) collective-permute-start(f32[4,128]{1,0:T(4,128)S(1)} %slice.7), channel_id=1, source_target_pairs={{0,16},{16,32},{32,48},{48,64},{64,80},{80,96},{96,112},{1,17},{17... | collective-permute-start | bytes 6152 | tf_op jit(solution)/shard_map/ppermute | solution.py:32
where the time goes:
time: 64.4 us; the launch traced here: 65.4 us
  Pallas kernels  25.9 us (40%)
  blocking collectives  24.8 us (39%)
  starting transfers between devices  7.37 us (11%)
  waiting for transfers between devices  5.96 us (9%)
  between operations  0.7 us (1%)
    all_to_all x1, blocking collectives, body(): received = lax.all_to_all(at_all, 'rank', 0, 0)  16.1 us
    pallas_call x1, Pallas kernels, body(): pl.pallas_call(own_kernel, out_shape=[jax.ShapeDtypeStruct((BLOCK, 128),...  12.6 us
    pallas_call x1, Pallas kernels, body(): pl.pallas_call(cross_kernel, out_shape=jax.ShapeDtypeStruct((RANKS, 8, 12...  11 us
    all_to_all x1, blocking collectives, body(): summed = jnp.sum(lax.all_to_all(partial, 'rank', 0, 0), axis=0)  8.69 us
    ppermute x2, starting transfers between devices, passed_along(): lax.ppermute(value, axis, [(source, source + steps) for source in range(l...  7.37 us
    ppermute x2, waiting for transfers between devices, passed_along(): lax.ppermute(value, axis, [(source, source + steps) for source in range(l...  5.96 us
    pallas_call x1, Pallas kernels, body(): pl.pallas_call(evaluate_kernel, out_shape=jax.ShapeDtypeStruct((RANKS, CH...  2.33 us
  transfers between devices with their start and end apart: 2, of which 1 were waited for; matrix products, arithmetic and copies ran while one was open for 0% of the time, Pallas kernels for 19%

commit v1 on v0

--- a/solution.py
+++ b/solution.py
@@ -1,5 +1,6 @@
 import jax
 import jax.numpy as jnp
+import ml_dtypes
 import numpy as np
 from jax import lax
 from jax.experimental import pallas as pl
@@ -14,7 +15,8 @@
 BLOCKS = 32
 SPAN = BLOCKS * BLOCK
 HELD = 512
-UNROLL = 8
+UNROLL = 16
+REST = 4
 LIST = 160
 LISTS = 512
 COUNTS = 480
@@ -43,7 +45,11 @@
     spread = np.zeros((RANKS, 16, 3, NCOEF), np.float32)
     for row, (time, coordinate) in enumerate(EIGHT + FOUR + FOUR):
         spread[:, row, coordinate, :] = table[time :: TIMES // RANKS]
-    return spread.reshape(RANKS * 16, 3 * NCOEF)
+    spread = spread.reshape(RANKS * 16, 3 * NCOEF)
+    high = spread.astype(ml_dtypes.bfloat16)
+    mid = (spread - high.astype(np.float32)).astype(ml_dtypes.bfloat16)
+    low = (spread - high.astype(np.float32) - mid.astype(np.float32)).astype(ml_dtypes.bfloat16)
+    return np.stack([np.concatenate([high, mid], axis=1), np.concatenate([high, low], axis=1)])
 
 
 def evaluate_kernel(*refs):
@@ -54,9 +60,12 @@
     for copy in copies:
         copy.wait()
     pairs, count, table, coefs, radii = held
-    values = jnp.dot(
-        table[...], coefs[...].reshape(3 * NCOEF, HELD), precision=lax.Precision.HIGHEST, preferred_element_type=F32
-    ).reshape(RANKS, 16, HELD)
+    high, mid, low = pieces(coefs[...].reshape(3 * NCOEF, HELD))
+    values = None
+    for which, above, below in ((0, high, high), (0, mid, mid), (1, low, high)):
+        part = jnp.dot(table[which], jnp.concatenate([above, below], axis=0), preferred_element_type=F32)
+        values = part if values is None else values + part
+    values = values.reshape(RANKS, 16, HELD)
     lane = lax.broadcasted_iota(jnp.int32, (1, 128), 1)
     row = lax.broadcasted_iota(jnp.int32, (8, 128), 0)
     last = jnp.where(row == 6, count[0].astype(F32), 0.0)
@@ -201,11 +210,18 @@
 
 
 def credit_list(first, first_radii, second, second_radii, rows, columns, lists, which):
-    @pl.loop(0, (lists[0, COUNTS + which] + UNROLL - 1) // UNROLL)
-    def _(step):
-        for u in range(UNROLL):
-            at = which * LIST + step * UNROLL + u
-            credit_pair(first, first_radii, second, second_radii, rows, columns, lists[0, at], lists[1, at])
+    count = lists[0, COUNTS + which]
+    whole = count // UNROLL
+
+    def steps(start, stop, pairs):
+        @pl.loop(start, stop)
+        def _(step):
+            for u in range(pairs):
+                at = which * LIST + step * pairs + u
+                credit_pair(first, first_radii, second, second_radii, rows, columns, lists[0, at], lists[1, at])
+
+    steps(0, whole, UNROLL)
+    steps(whole * (UNROLL // REST), (count + REST - 1) // REST, REST)
 
 
 def block_sums(columns):
@@ -261,7 +277,7 @@
         scratch_shapes=[
             SMEM(pair_blocks.shape, jnp.int32),
             SMEM(pair_count.shape, jnp.int32),
-            VMEM(table.shape, F32),
+            VMEM(table.shape, BF16),
             VMEM(coefs.shape, F32),
             VMEM(radii.shape, F32),
             pltpu.SemaphoreType.DMA((5,)),

time: 64.4 us -> 61.1 us (0.949)
  Pallas kernels: 25.9 us -> 19.6 us
  starting transfers between devices: 7.37 us -> 9.32 us
    pallas_call x1, Pallas kernels: 12.6 us -> 7.88 us  [body(): pl.pallas_call(own_kernel, out_shape=[jax.ShapeDtypeStruct((BLOCK, 128),...]
    ppermute x2, starting transfers between devices: 7.37 us -> 9.32 us  [passed_along(): lax.ppermute(value, axis, [(source, source + steps) for source in range(l...]
    pallas_call x1, Pallas kernels: 11 us -> 9.63 us  [body(): pl.pallas_call(cross_kernel, out_shape=jax.ShapeDtypeStruct((RANKS, 8, 12...]
  transfers between devices with their start and end apart: 2 -> 2, of which waited for: 1 -> 2; matrix products, arithmetic and copies ran while one was open for 0% -> 0% of each run, Pallas kernels for 19% -> 13%
where the time goes in v1:
time: 61.1 us; the launch traced here: 61.4 us
  blocking collectives  25.2 us (41%)
  Pallas kernels  19.6 us (32%)
  starting transfers between devices  9.32 us (15%)
  waiting for transfers between devices  5.99 us (10%)
  between operations  0.69 us (1%)
    all_to_all x1, blocking collectives, body(): received = lax.all_to_all(at_all, 'rank', 0, 0)  16.1 us
    pallas_call x1, Pallas kernels, body(): pl.pallas_call(cross_kernel, out_shape=jax.ShapeDtypeStruct((RANKS, 8, 12...  9.63 us
    ppermute x2, starting transfers between devices, passed_along(): lax.ppermute(value, axis, [(source, source + steps) for source in range(l...  9.32 us
    all_to_all x1, blocking collectives, body(): summed = jnp.sum(lax.all_to_all(partial, 'rank', 0, 0), axis=0)  9.09 us
    pallas_call x1, Pallas kernels, body(): pl.pallas_call(own_kernel, out_shape=[jax.ShapeDtypeStruct((BLOCK, 128),...  7.88 us
    ppermute x2, waiting for transfers between devices, passed_along(): lax.ppermute(value, axis, [(source, source + steps) for source in range(l...  5.99 us
    pallas_call x1, Pallas kernels, body(): pl.pallas_call(evaluate_kernel, out_shape=jax.ShapeDtypeStruct((RANKS, CH...  2.13 us
  transfers between devices with their start and end apart: 2, of which 2 were waited for; matrix products, arithmetic and copies ran while one was open for 0% of the time, Pallas kernels for 13%

profile of v1, /device:TPU:4, one launch (start us, length us, event | category | flops | bytes accessed | tf_op | source)
XLA Modules:
  0.0 61.4 jit_solution(9437939033308419763)
XLA Ops:
  0.7 2.1 %evaluate.1 = f32[16,56,128]{2,1,0:T(8,128)} custom-call(s32[2,8]{1,0:T(2,128)} %refs_0_.1, s32[1]{0:T(128)S(6)} %copy.6.refs_1_, bf16[2,256,96]{2,1,0:T(8,128)(2,1)} %constant.4.clone.refs_2_, f32[3,16,512]{2,1,0:T(8,128)} %bitcast.3, f32[512]{0:T(512)} %refs_4_.1), custom_call_target="tpu_custom_call" | custom-call | tf_op jit(solution)/shard_map/evaluate/pallas_call | solution.py:272
  2.8 16.1 %all_to_all.10.received = f32[16,56,128]{2,1,0:T(8,128)S(1)} all-to-all(f32[16,56,128]{2,1,0:T(8,128)} %evaluate.1), channel_id=1, replica_groups=mesh['shell'=8,'rank'=16] {'rank'}, dimensions={0} | all-to-all | bytes 917504 | tf_op jit(solution)/shard_map/all_to_all | solution.py:288
  18.9 5.5 %collective-permute-start = (f32[16,56,128]{2,1,0:T(8,128)S(1)}, f32[16,56,128]{2,1,0:T(8,128)S(1)}, u32[]{:S(2)}, u32[]{:S(2)}) collective-permute-start(f32[16,56,128]{2,1,0:T(8,128)S(1)} %all_to_all.10.received), channel_id=1, source_target_pairs={{16,0},{32,16},{48,32},{64,48},{80,64},{96,80},{112,96},{17,1},{33... | collective-permute-start | bytes 1376264 | tf_op jit(solution)/shard_map/ppermute | solution.py:34
  24.3 7.9 %own_pairs.1 = (f32[256,128]{1,0:T(8,128)S(1)}, f32[32,256]{1,0:T(8,128)S(1)}, bf16[8192,128]{1,0:T(8,128)(2,1)S(1)}, f32[8192,128]{1,0:T(8,128)S(1)}, s32[2,512]{1,0:T(2,128)S(1)}) custom-call(f32[16,56,128]{2,1,0:T(8,128)S(1)} %all_to_all.10.received), custom_call_target="tpu_custom_call" | custom-call | flops 8000000000 | bytes 8000000 | tf_op jit(solution)/shard_map/own_pairs/pallas_call | solution.py:290
  32.2 2.0 %collective-permute-done.received = f32[16,56,128]{2,1,0:T(8,128)S(1)} collective-permute-done((f32[16,56,128]{2,1,0:T(8,128)S(1)}, f32[16,56,128]{2,1,0:T(8,128)S(1)}, u32[]{:S(2)}, u32[]{:S(2)}) %collective-permute-start) | collective-permute-done | bytes 458784 | tf_op jit(solution)/shard_map/ppermute | solution.py:34
  34.2 9.6 %crossing_pairs.1 = f32[16,8,128]{2,1,0:T(8,128)S(1)} custom-call(s32[2,512]{1,0:T(2,128)S(1)} %get-tuple-element.10.lists, f32[16,56,128]{2,1,0:T(8,128)S(1)} %collective-permute-done.received, f32[256,128]{1,0:T(8,128)S(1)} %get-tuple-element.11.earlier_rows, f32[32,256]{1,0:T(8,128)S(1)} %get-tuple-element.12.earlier, ...), custom_call_target="tpu_custom_call" | custom-call | flops 8000000000 | bytes 8000000 | tf_op jit(solution)/shard_map/crossing_pairs/pallas_call | solution.py:312
  43.9 9.1 %all_to_all.11 = f32[16,8,128]{2,1,0:T(8,128)S(1)} all-to-all(f32[16,8,128]{2,1,0:T(8,128)S(1)} %crossing_pairs.1), channel_id=1, replica_groups=mesh['shell'=8,'rank'=16] {'rank'}, dimensions={0} | all-to-all | bytes 131072 | tf_op jit(solution)/shard_map/all_to_all | solution.py:327
  53.0 3.9 %collective-permute-start.1 = (f32[4,128]{1,0:T(4,128)S(1)}, f32[4,128]{1,0:T(4,128)S(1)}, u32[]{:S(2)}, u32[]{:S(2)}) collective-permute-start(f32[4,128]{1,0:T(4,128)S(1)} %slice.7), channel_id=1, source_target_pairs={{0,16},{16,32},{32,48},{48,64},{64,80},{80,96},{96,112},{1,17},{17... | collective-permute-start | bytes 6152 | tf_op jit(solution)/shard_map/ppermute | solution.py:34
  56.9 4.0 %collective-permute-done.1 = f32[4,128]{1,0:T(4,128)S(1)} collective-permute-done((f32[4,128]{1,0:T(4,128)S(1)}, f32[4,128]{1,0:T(4,128)S(1)}, u32[]{:S(2)}, u32[]{:S(2)}) %collective-permute-start.1) | collective-permute-done | bytes 2080 | tf_op jit(solution)/shard_map/ppermute | solution.py:34
  60.9 0.6 add_bitcast_fusion
  (2 shorter events, 0.0 us)
Async XLA Ops:
  18.9 15.3 %collective-permute-start = (f32[16,56,128]{2,1,0:T(8,128)S(1)}, f32[16,56,128]{2,1,0:T(8,128)S(1)}, u32[]{:S(2)}, u32[]{:S(2)}) collective-permute-start(f32[16,56,128]{2,1,0:T(8,128)S(1)} %all_to_all.10.received), channel_id=1, source_target_pairs={{16,0},{32,16},{48,32},{64,48},{80,64},{96,80},{112,96},{17,1},{33... | collective-permute-start | bytes 1376264 | tf_op jit(solution)/shard_map/ppermute | solution.py:34
  53.0 7.9 %collective-permute-start.1 = (f32[4,128]{1,0:T(4,128)S(1)}, f32[4,128]{1,0:T(4,128)S(1)}, u32[]{:S(2)}, u32[]{:S(2)}) collective-permute-start(f32[4,128]{1,0:T(4,128)S(1)} %slice.7), channel_id=1, source_target_pairs={{0,16},{16,32},{32,48},{48,64},{64,80},{80,96},{96,112},{1,17},{17... | collective-permute-start | bytes 6152 | tf_op jit(solution)/shard_map/ppermute | solution.py:34

commit v2 on v1

--- a/solution.py
+++ b/solution.py
@@ -247,13 +247,16 @@
 
 def cross_kernel(
     lists, received, earlier_rows, earlier, first, first_radii, out,
-    second, second_radii, rows, columns,
+    second, second_radii, rows, columns, listed, sem,
 ):
+    copy = pltpu.make_async_copy(lists, listed, sem)
+    copy.start()
     rows[...] = earlier_rows[...]
     columns[...] = jnp.zeros_like(columns)
     for rank in range(RANKS):
         prepare_second(second, second_radii, received, rank)
-    credit_list(first, first_radii, second, second_radii, rows, columns, lists, 1)
+    copy.wait()
+    credit_list(first, first_radii, second, second_radii, rows, columns, listed, 1)
     factor = 1.0 / (TIMES * BLOCK)
     own = (earlier[...] + rows[...].T[0:BLOCKS, :]) * factor
     beyond = block_sums(columns) * factor
@@ -266,7 +269,7 @@
 
 
 def body(coefs, radii, pair_blocks, pair_count):
-    in_vmem, in_smem = pl.BlockSpec(memory_space=VMEM), pl.BlockSpec(memory_space=SMEM)
+    in_vmem = pl.BlockSpec(memory_space=VMEM)
     table = jnp.asarray(spread_table())
     coefs = coefs.transpose(1, 0, 2)
     at_all = pl.pallas_call(
@@ -312,13 +315,15 @@
     partial = pl.pallas_call(
         cross_kernel,
         out_shape=jax.ShapeDtypeStruct((RANKS, 8, 128), F32),
-        in_specs=[in_smem] + [in_vmem] * 5,
+        in_specs=[in_vmem] * 6,
         out_specs=in_vmem,
         scratch_shapes=[
             VMEM((128, SPAN), BF16),
             VMEM((BLOCKS, BLOCK), F32),
             VMEM((BLOCK, 128), F32),
             VMEM((8 * BLOCKS + 8, BLOCK), F32),
+            SMEM((2, LISTS), jnp.int32),
+            pltpu.SemaphoreType.DMA,
         ],
         compiler_params=PARAMS,
         cost_estimate=pl.CostEstimate(flops=8_000_000_000, bytes_accessed=8_000_000, transcendentals=0),

time: 61.1 us -> 61.1 us (level)
  the two profiles are of different devices: /device:TPU:4 before, /device:TPU:2 now
where the time goes in v2:
time: 61.1 us; the launch traced here: 61 us
  blocking collectives  24.8 us (41%)
  Pallas kernels  21.6 us (35%)
  starting transfers between devices  8.44 us (14%)
  waiting for transfers between devices  4.89 us (8%)
  between operations  0.7 us (1%)
    all_to_all x1, blocking collectives, body(): received = lax.all_to_all(at_all, 'rank', 0, 0)  16.1 us
    pallas_call x1, Pallas kernels, body(): pl.pallas_call(own_kernel, out_shape=[jax.ShapeDtypeStruct((BLOCK, 128),...  11.2 us
    all_to_all x1, blocking collectives, body(): summed = jnp.sum(lax.all_to_all(partial, 'rank', 0, 0), axis=0)  8.69 us
    ppermute x2, starting transfers between devices, passed_along(): lax.ppermute(value, axis, [(source, source + steps) for source in range(l...  8.44 us
    pallas_call x1, Pallas kernels, body(): pl.pallas_call(cross_kernel, out_shape=jax.ShapeDtypeStruct((RANKS, 8, 12...  8.3 us
    ppermute x2, waiting for transfers between devices, passed_along(): lax.ppermute(value, axis, [(source, source + steps) for source in range(l...  4.89 us
    pallas_call x1, Pallas kernels, body(): pl.pallas_call(evaluate_kernel, out_shape=jax.ShapeDtypeStruct((RANKS, CH...  2.13 us
  transfers between devices with their start and end apart: 2, of which 1 were waited for; matrix products, arithmetic and copies ran while one was open for 0% of the time, Pallas kernels for 18%

profile of v2, /device:TPU:2, one launch (start us, length us, event | category | flops | bytes accessed | tf_op | source)
XLA Modules:
  0.0 61.0 jit_solution(7681427800084141992)
XLA Ops:
  0.7 2.1 %evaluate.1 = f32[16,56,128]{2,1,0:T(8,128)} custom-call(s32[2,8]{1,0:T(2,128)} %refs_0_.1, s32[1]{0:T(128)S(6)} %copy.6.refs_1_, bf16[2,256,96]{2,1,0:T(8,128)(2,1)} %constant.4.clone.refs_2_, f32[3,16,512]{2,1,0:T(8,128)} %bitcast.3, f32[512]{0:T(512)} %refs_4_.1), custom_call_target="tpu_custom_call" | custom-call | tf_op jit(solution)/shard_map/evaluate/pallas_call | solution.py:275
  2.8 16.1 %all_to_all.10.received = f32[16,56,128]{2,1,0:T(8,128)S(1)} all-to-all(f32[16,56,128]{2,1,0:T(8,128)} %evaluate.1), channel_id=1, replica_groups=mesh['shell'=8,'rank'=16] {'rank'}, dimensions={0} | all-to-all | bytes 917504 | tf_op jit(solution)/shard_map/all_to_all | solution.py:291
  18.9 5.5 %collective-permute-start = (f32[16,56,128]{2,1,0:T(8,128)S(1)}, f32[16,56,128]{2,1,0:T(8,128)S(1)}, u32[]{:S(2)}, u32[]{:S(2)}) collective-permute-start(f32[16,56,128]{2,1,0:T(8,128)S(1)} %all_to_all.10.received), channel_id=1, source_target_pairs={{16,0},{32,16},{48,32},{64,48},{80,64},{96,80},{112,96},{17,1},{33... | collective-permute-start | bytes 1376264 | tf_op jit(solution)/shard_map/ppermute | solution.py:34
  24.3 11.2 %own_pairs.1 = (f32[256,128]{1,0:T(8,128)S(1)}, f32[32,256]{1,0:T(8,128)S(1)}, bf16[8192,128]{1,0:T(8,128)(2,1)S(1)}, f32[8192,128]{1,0:T(8,128)S(1)}, s32[2,512]{1,0:T(2,128)S(1)}) custom-call(f32[16,56,128]{2,1,0:T(8,128)S(1)} %all_to_all.10.received), custom_call_target="tpu_custom_call" | custom-call | flops 8000000000 | bytes 8000000 | tf_op jit(solution)/shard_map/own_pairs/pallas_call | solution.py:293
  35.5 0.0 collective-permute-done.received
  35.5 8.3 %crossing_pairs.1 = f32[16,8,128]{2,1,0:T(8,128)S(1)} custom-call(s32[2,512]{1,0:T(2,128)S(1)} %get-tuple-element.10.lists, f32[16,56,128]{2,1,0:T(8,128)S(1)} %collective-permute-done.received, f32[256,128]{1,0:T(8,128)S(1)} %get-tuple-element.11.earlier_rows, f32[32,256]{1,0:T(8,128)S(1)} %get-tuple-element.12.earlier, ...), custom_call_target="tpu_custom_call" | custom-call | flops 8000000000 | bytes 8000000 | tf_op jit(solution)/shard_map/crossing_pairs/pallas_call | solution.py:315
  43.8 8.7 %all_to_all.11 = f32[16,8,128]{2,1,0:T(8,128)S(1)} all-to-all(f32[16,8,128]{2,1,0:T(8,128)S(1)} %crossing_pairs.1), channel_id=1, replica_groups=mesh['shell'=8,'rank'=16] {'rank'}, dimensions={0} | all-to-all | bytes 131072 | tf_op jit(solution)/shard_map/all_to_all | solution.py:332
  52.6 3.0 %collective-permute-start.1 = (f32[4,128]{1,0:T(4,128)S(1)}, f32[4,128]{1,0:T(4,128)S(1)}, u32[]{:S(2)}, u32[]{:S(2)}) collective-permute-start(f32[4,128]{1,0:T(4,128)S(1)} %slice.7), channel_id=1, source_target_pairs={{0,16},{16,32},{32,48},{48,64},{64,80},{80,96},{96,112},{1,17},{17... | collective-permute-start | bytes 6152 | tf_op jit(solution)/shard_map/ppermute | solution.py:34
  55.6 4.9 %collective-permute-done.1 = f32[4,128]{1,0:T(4,128)S(1)} collective-permute-done((f32[4,128]{1,0:T(4,128)S(1)}, f32[4,128]{1,0:T(4,128)S(1)}, u32[]{:S(2)}, u32[]{:S(2)}) %collective-permute-start.1) | collective-permute-done | bytes 2080 | tf_op jit(solution)/shard_map/ppermute | solution.py:34
  60.4 0.6 add_bitcast_fusion
  (2 shorter events, 0.0 us)
Async XLA Ops:
  18.9 16.6 %collective-permute-start = (f32[16,56,128]{2,1,0:T(8,128)S(1)}, f32[16,56,128]{2,1,0:T(8,128)S(1)}, u32[]{:S(2)}, u32[]{:S(2)}) collective-permute-start(f32[16,56,128]{2,1,0:T(8,128)S(1)} %all_to_all.10.received), channel_id=1, source_target_pairs={{16,0},{32,16},{48,32},{64,48},{80,64},{96,80},{112,96},{17,1},{33... | collective-permute-start | bytes 1376264 | tf_op jit(solution)/shard_map/ppermute | solution.py:34
  52.6 7.9 %collective-permute-start.1 = (f32[4,128]{1,0:T(4,128)S(1)}, f32[4,128]{1,0:T(4,128)S(1)}, u32[]{:S(2)}, u32[]{:S(2)}) collective-permute-start(f32[4,128]{1,0:T(4,128)S(1)} %slice.7), channel_id=1, source_target_pairs={{0,16},{16,32},{32,48},{48,64},{64,80},{80,96},{96,112},{1,17},{17... | collective-permute-start | bytes 6152 | tf_op jit(solution)/shard_map/ppermute | solution.py:34

commit v3 on v2

--- a/solution.py
+++ b/solution.py
@@ -53,13 +53,14 @@
 
 
 def evaluate_kernel(*refs):
-    given, (out, *held, sems) = refs[:5], refs[5:]
-    copies = [pltpu.make_async_copy(given[i], held[i], sems.at[i]) for i in range(5)]
+    count, *given = refs[:5]
+    out, *held, sems = refs[5:]
+    copies = [pltpu.make_async_copy(given[i], held[i], sems.at[i]) for i in range(4)]
     for copy in copies:
         copy.start()
     for copy in copies:
         copy.wait()
-    pairs, count, table, coefs, radii = held
+    pairs, table, coefs, radii = held
     high, mid, low = pieces(coefs[...].reshape(3 * NCOEF, HELD))
     values = None
     for which, above, below in ((0, high, high), (0, mid, mid), (1, low, high)):
@@ -275,19 +276,18 @@
     at_all = pl.pallas_call(
         evaluate_kernel,
         out_shape=jax.ShapeDtypeStruct((RANKS, CHUNK, 128), F32),
-        in_specs=[pl.BlockSpec(memory_space=pltpu.HBM)] * 5,
+        in_specs=[pl.BlockSpec(memory_space=SMEM)] + [pl.BlockSpec(memory_space=pltpu.HBM)] * 4,
         out_specs=in_vmem,
         scratch_shapes=[
             SMEM(pair_blocks.shape, jnp.int32),
-            SMEM(pair_count.shape, jnp.int32),
             VMEM(table.shape, BF16),
             VMEM(coefs.shape, F32),
             VMEM(radii.shape, F32),
-            pltpu.SemaphoreType.DMA((5,)),
+            pltpu.SemaphoreType.DMA((4,)),
         ],
-        compiler_params=pltpu.CompilerParams(vmem_limit_bytes=60 * 1024 * 1024),
+        compiler_params=PARAMS,
         name="evaluate",
-    )(pair_blocks, pair_count, table, coefs, radii)
+    )(pair_count, *(pltpu.with_memory_space_constraint(x, pltpu.HBM) for x in (pair_blocks, table, coefs, radii)))
     received = lax.all_to_all(at_all, "rank", 0, 0)
     beyond = passed_along(received, "shell", -1)
     rows, credited, first, first_radii, lists = pl.pallas_call(

time: 61.1 us -> 60.4 us (0.989)
  the two profiles are of different devices: /device:TPU:2 before, /device:TPU:4 now
where the time goes in v3:
time: 60.4 us; the launch traced here: 59.3 us
  blocking collectives  25 us (41%)
  Pallas kernels  16.8 us (28%)
  starting transfers between devices  11.7 us (19%)
  waiting for transfers between devices  4.5 us (7%)
  between operations  0.69 us (1%)
    all_to_all x1, blocking collectives, body(): received = lax.all_to_all(at_all, 'rank', 0, 0)  15.9 us
    ppermute x2, starting transfers between devices, passed_along(): lax.ppermute(value, axis, [(source, source + steps) for source in range(l...  11.7 us
    all_to_all x1, blocking collectives, body(): summed = jnp.sum(lax.all_to_all(partial, 'rank', 0, 0), axis=0)  9.1 us
    pallas_call x1, Pallas kernels, body(): pl.pallas_call(own_kernel, out_shape=[jax.ShapeDtypeStruct((BLOCK, 128),...  8.75 us
    pallas_call x1, Pallas kernels, body(): pl.pallas_call(cross_kernel, out_shape=jax.ShapeDtypeStruct((RANKS, 8, 12...  6.71 us
    ppermute x2, waiting for transfers between devices, passed_along(): lax.ppermute(value, axis, [(source, source + steps) for source in range(l...  4.5 us
    pallas_call x1, Pallas kernels, body(): pl.pallas_call(evaluate_kernel, out_shape=jax.ShapeDtypeStruct((RANKS, CH...  1.35 us
  transfers between devices with their start and end apart: 2, of which 2 were waited for; matrix products, arithmetic and copies ran while one was open for 0% of the time, Pallas kernels for 15%

profile of v3, /device:TPU:4, one launch (start us, length us, event | category | flops | bytes accessed | tf_op | source)
XLA Modules:
  0.0 59.3 jit_solution(13764425134909913225)
XLA Ops:
  0.7 1.4 %evaluate.1 = f32[16,56,128]{2,1,0:T(8,128)S(1)} custom-call(s32[1]{0:T(128)S(6)} %copy.6.refs_0_, s32[2,8]{1,0:T(2,128)} %refs_1_.1, bf16[2,256,96]{2,1,0:T(8,128)(2,1)} %constant.4.clone.refs_2_, f32[3,16,512]{2,1,0:T(8,128)} %bitcast.3, f32[512]{0:T(512)} %refs_4_.1), custom_call_target="tpu_custom_call" | custom-call | tf_op jit(solution)/shard_map/evaluate/pallas_call | solution.py:276
  2.0 15.9 %all_to_all.10.received = f32[16,56,128]{2,1,0:T(8,128)S(1)} all-to-all(f32[16,56,128]{2,1,0:T(8,128)S(1)} %evaluate.1), channel_id=1, replica_groups=mesh['shell'=8,'rank'=16] {'rank'}, dimensions={0} | all-to-all | bytes 917504 | tf_op jit(solution)/shard_map/all_to_all | solution.py:291
  17.9 5.5 %collective-permute-start = (f32[16,56,128]{2,1,0:T(8,128)S(1)}, f32[16,56,128]{2,1,0:T(8,128)S(1)}, u32[]{:S(2)}, u32[]{:S(2)}) collective-permute-start(f32[16,56,128]{2,1,0:T(8,128)S(1)} %all_to_all.10.received), channel_id=1, source_target_pairs={{16,0},{32,16},{48,32},{64,48},{80,64},{96,80},{112,96},{17,1},{33... | collective-permute-start | bytes 1376264 | tf_op jit(solution)/shard_map/ppermute | solution.py:34
  23.4 8.8 %own_pairs.1 = (f32[256,128]{1,0:T(8,128)S(1)}, f32[32,256]{1,0:T(8,128)S(1)}, bf16[8192,128]{1,0:T(8,128)(2,1)S(1)}, f32[8192,128]{1,0:T(8,128)S(1)}, s32[2,512]{1,0:T(2,128)S(1)}) custom-call(f32[16,56,128]{2,1,0:T(8,128)S(1)} %all_to_all.10.received), custom_call_target="tpu_custom_call" | custom-call | flops 8000000000 | bytes 8000000 | tf_op jit(solution)/shard_map/own_pairs/pallas_call | solution.py:293
  32.1 1.1 %collective-permute-done.received = f32[16,56,128]{2,1,0:T(8,128)S(1)} collective-permute-done((f32[16,56,128]{2,1,0:T(8,128)S(1)}, f32[16,56,128]{2,1,0:T(8,128)S(1)}, u32[]{:S(2)}, u32[]{:S(2)}) %collective-permute-start) | collective-permute-done | bytes 458784 | tf_op jit(solution)/shard_map/ppermute | solution.py:34
  33.2 6.7 %crossing_pairs.1 = f32[16,8,128]{2,1,0:T(8,128)S(1)} custom-call(s32[2,512]{1,0:T(2,128)S(1)} %get-tuple-element.10.lists, f32[16,56,128]{2,1,0:T(8,128)S(1)} %collective-permute-done.received, f32[256,128]{1,0:T(8,128)S(1)} %get-tuple-element.11.earlier_rows, f32[32,256]{1,0:T(8,128)S(1)} %get-tuple-element.12.earlier, ...), custom_call_target="tpu_custom_call" | custom-call | flops 8000000000 | bytes 8000000 | tf_op jit(solution)/shard_map/crossing_pairs/pallas_call | solution.py:315
  40.0 9.1 %all_to_all.11 = f32[16,8,128]{2,1,0:T(8,128)S(1)} all-to-all(f32[16,8,128]{2,1,0:T(8,128)S(1)} %crossing_pairs.1), channel_id=1, replica_groups=mesh['shell'=8,'rank'=16] {'rank'}, dimensions={0} | all-to-all | bytes 131072 | tf_op jit(solution)/shard_map/all_to_all | solution.py:332
  49.1 6.2 %collective-permute-start.1 = (f32[4,128]{1,0:T(4,128)S(1)}, f32[4,128]{1,0:T(4,128)S(1)}, u32[]{:S(2)}, u32[]{:S(2)}) collective-permute-start(f32[4,128]{1,0:T(4,128)S(1)} %slice.7), channel_id=1, source_target_pairs={{0,16},{16,32},{32,48},{48,64},{64,80},{80,96},{96,112},{1,17},{17... | collective-permute-start | bytes 6152 | tf_op jit(solution)/shard_map/ppermute | solution.py:34
  55.3 3.4 %collective-permute-done.1 = f32[4,128]{1,0:T(4,128)S(1)} collective-permute-done((f32[4,128]{1,0:T(4,128)S(1)}, f32[4,128]{1,0:T(4,128)S(1)}, u32[]{:S(2)}, u32[]{:S(2)}) %collective-permute-start.1) | collective-permute-done | bytes 2080 | tf_op jit(solution)/shard_map/ppermute | solution.py:34
  58.7 0.6 add_bitcast_fusion
  (2 shorter events, 0.0 us)
Async XLA Ops:
  17.9 15.3 %collective-permute-start = (f32[16,56,128]{2,1,0:T(8,128)S(1)}, f32[16,56,128]{2,1,0:T(8,128)S(1)}, u32[]{:S(2)}, u32[]{:S(2)}) collective-permute-start(f32[16,56,128]{2,1,0:T(8,128)S(1)} %all_to_all.10.received), channel_id=1, source_target_pairs={{16,0},{32,16},{48,32},{64,48},{80,64},{96,80},{112,96},{17,1},{33... | collective-permute-start | bytes 1376264 | tf_op jit(solution)/shard_map/ppermute | solution.py:34
  49.1 9.6 %collective-permute-start.1 = (f32[4,128]{1,0:T(4,128)S(1)}, f32[4,128]{1,0:T(4,128)S(1)}, u32[]{:S(2)}, u32[]{:S(2)}) collective-permute-start(f32[4,128]{1,0:T(4,128)S(1)} %slice.7), channel_id=1, source_target_pairs={{0,16},{16,32},{32,48},{48,64},{64,80},{80,96},{96,112},{1,17},{17... | collective-permute-start | bytes 6152 | tf_op jit(solution)/shard_map/ppermute | solution.py:34

commit v4 on v3

--- a/solution.py
+++ b/solution.py
@@ -15,8 +15,7 @@
 BLOCKS = 32
 SPAN = BLOCKS * BLOCK
 HELD = 512
-UNROLL = 16
-REST = 4
+STEPS = (24, 8, 4)
 LIST = 160
 LISTS = 512
 COUNTS = 480
@@ -56,12 +55,13 @@
     count, *given = refs[:5]
     out, *held, sems = refs[5:]
     copies = [pltpu.make_async_copy(given[i], held[i], sems.at[i]) for i in range(4)]
-    for copy in copies:
-        copy.start()
-    for copy in copies:
-        copy.wait()
     pairs, table, coefs, radii = held
+    for i in (2, 1, 0, 3):
+        copies[i].start()
+    copies[2].wait()
     high, mid, low = pieces(coefs[...].reshape(3 * NCOEF, HELD))
+    for i in (1, 0, 3):
+        copies[i].wait()
     values = None
     for which, above, below in ((0, high, high), (0, mid, mid), (1, low, high)):
         part = jnp.dot(table[which], jnp.concatenate([above, below], axis=0), preferred_element_type=F32)
@@ -212,17 +212,17 @@
 
 def credit_list(first, first_radii, second, second_radii, rows, columns, lists, which):
     count = lists[0, COUNTS + which]
-    whole = count // UNROLL
-
-    def steps(start, stop, pairs):
-        @pl.loop(start, stop)
+    done = jnp.int32(0)
+    for pairs in STEPS:
+        steps = jnp.maximum(count - done + 3, 0) // pairs
+
+        @pl.loop(0, steps)
         def _(step):
             for u in range(pairs):
-                at = which * LIST + step * pairs + u
+                at = which * LIST + done + step * pairs + u
                 credit_pair(first, first_radii, second, second_radii, rows, columns, lists[0, at], lists[1, at])
 
-    steps(0, whole, UNROLL)
-    steps(whole * (UNROLL // REST), (count + REST - 1) // REST, REST)
+        done = done + steps * pairs
 
 
 def block_sums(columns):

time: 60.4 us -> 59.5 us (0.985); the launches traced: 59.3 us -> 59.1 us
  Pallas kernels: 16.8 us -> 18.4 us
  waiting for transfers between devices: 4.5 us -> 3.46 us
  starting transfers between devices: 11.7 us -> 11 us
    pallas_call x1, Pallas kernels: 6.71 us -> 8.31 us  [body(): pl.pallas_call(cross_kernel, out_shape=jax.ShapeDtypeStruct((RANKS, 8, 12...]
    ppermute x2, waiting for transfers between devices: 4.5 us -> 3.46 us  [passed_along(): lax.ppermute(value, axis, [(source, source + steps) for source in range(l...]
    ppermute x2, starting transfers between devices: 11.7 us -> 11 us  [passed_along(): lax.ppermute(value, axis, [(source, source + steps) for source in range(l...]
where the time goes in v4:
time: 59.5 us; the launch traced here: 59.1 us
  blocking collectives  25 us (42%)
  Pallas kernels  18.4 us (31%)
  starting transfers between devices  11 us (18%)
  waiting for transfers between devices  3.46 us (6%)
  between operations  0.7 us (1%)
  other arithmetic  0.6 us (1%)
    all_to_all x1, blocking collectives, body(): received = lax.all_to_all(at_all, 'rank', 0, 0)  15.9 us
    ppermute x2, starting transfers between devices, passed_along(): lax.ppermute(value, axis, [(source, source + steps) for source in range(l...  11 us
    all_to_all x1, blocking collectives, body(): summed = jnp.sum(lax.all_to_all(partial, 'rank', 0, 0), axis=0)  9.1 us
    pallas_call x1, Pallas kernels, body(): pl.pallas_call(own_kernel, out_shape=[jax.ShapeDtypeStruct((BLOCK, 128),...  8.78 us
    pallas_call x1, Pallas kernels, body(): pl.pallas_call(cross_kernel, out_shape=jax.ShapeDtypeStruct((RANKS, 8, 12...  8.31 us
    ppermute x2, waiting for transfers between devices, passed_along(): lax.ppermute(value, axis, [(source, source + steps) for source in range(l...  3.46 us
    pallas_call x1, Pallas kernels, body(): pl.pallas_call(evaluate_kernel, out_shape=jax.ShapeDtypeStruct((RANKS, CH...  1.34 us
  transfers between devices with their start and end apart: 2, of which 2 were waited for; matrix products, arithmetic and copies ran while one was open for 0% of the time, Pallas kernels for 15%

profile of v4, /device:TPU:4, one launch (start us, length us, event | category | flops | bytes accessed | tf_op | source)
XLA Modules:
  0.0 59.1 jit_solution(12125950953130441283)
XLA Ops:
  0.7 1.3 %evaluate.1 = f32[16,56,128]{2,1,0:T(8,128)S(1)} custom-call(s32[1]{0:T(128)S(6)} %copy.6.refs_0_, s32[2,8]{1,0:T(2,128)} %refs_1_.1, bf16[2,256,96]{2,1,0:T(8,128)(2,1)} %constant.4.clone.refs_2_, f32[3,16,512]{2,1,0:T(8,128)} %bitcast.3, f32[512]{0:T(512)} %refs_4_.1), custom_call_target="tpu_custom_call" | custom-call | tf_op jit(solution)/shard_map/evaluate/pallas_call | solution.py:276
  2.0 15.9 %all_to_all.10.received = f32[16,56,128]{2,1,0:T(8,128)S(1)} all-to-all(f32[16,56,128]{2,1,0:T(8,128)S(1)} %evaluate.1), channel_id=1, replica_groups=mesh['shell'=8,'rank'=16] {'rank'}, dimensions={0} | all-to-all | bytes 917504 | tf_op jit(solution)/shard_map/all_to_all | solution.py:291
  17.9 5.4 %collective-permute-start = (f32[16,56,128]{2,1,0:T(8,128)S(1)}, f32[16,56,128]{2,1,0:T(8,128)S(1)}, u32[]{:S(2)}, u32[]{:S(2)}) collective-permute-start(f32[16,56,128]{2,1,0:T(8,128)S(1)} %all_to_all.10.received), channel_id=1, source_target_pairs={{16,0},{32,16},{48,32},{64,48},{80,64},{96,80},{112,96},{17,1},{33... | collective-permute-start | bytes 1376264 | tf_op jit(solution)/shard_map/ppermute | solution.py:33
  23.3 8.8 %own_pairs.1 = (f32[256,128]{1,0:T(8,128)S(1)}, f32[32,256]{1,0:T(8,128)S(1)}, bf16[8192,128]{1,0:T(8,128)(2,1)S(1)}, f32[8192,128]{1,0:T(8,128)S(1)}, s32[2,512]{1,0:T(2,128)S(1)}) custom-call(f32[16,56,128]{2,1,0:T(8,128)S(1)} %all_to_all.10.received), custom_call_target="tpu_custom_call" | custom-call | flops 8000000000 | bytes 8000000 | tf_op jit(solution)/shard_map/own_pairs/pallas_call | solution.py:293
  32.1 1.1 %collective-permute-done.received = f32[16,56,128]{2,1,0:T(8,128)S(1)} collective-permute-done((f32[16,56,128]{2,1,0:T(8,128)S(1)}, f32[16,56,128]{2,1,0:T(8,128)S(1)}, u32[]{:S(2)}, u32[]{:S(2)}) %collective-permute-start) | collective-permute-done | bytes 458784 | tf_op jit(solution)/shard_map/ppermute | solution.py:33
  33.2 8.3 %crossing_pairs.1 = f32[16,8,128]{2,1,0:T(8,128)S(1)} custom-call(s32[2,512]{1,0:T(2,128)S(1)} %get-tuple-element.10.lists, f32[16,56,128]{2,1,0:T(8,128)S(1)} %collective-permute-done.received, f32[256,128]{1,0:T(8,128)S(1)} %get-tuple-element.11.earlier_rows, f32[32,256]{1,0:T(8,128)S(1)} %get-tuple-element.12.earlier, ...), custom_call_target="tpu_custom_call" | custom-call | flops 8000000000 | bytes 8000000 | tf_op jit(solution)/shard_map/crossing_pairs/pallas_call | solution.py:315
  41.5 9.1 %all_to_all.11 = f32[16,8,128]{2,1,0:T(8,128)S(1)} all-to-all(f32[16,8,128]{2,1,0:T(8,128)S(1)} %crossing_pairs.1), channel_id=1, replica_groups=mesh['shell'=8,'rank'=16] {'rank'}, dimensions={0} | all-to-all | bytes 131072 | tf_op jit(solution)/shard_map/all_to_all | solution.py:332
  50.7 5.5 %collective-permute-start.1 = (f32[4,128]{1,0:T(4,128)S(1)}, f32[4,128]{1,0:T(4,128)S(1)}, u32[]{:S(2)}, u32[]{:S(2)}) collective-permute-start(f32[4,128]{1,0:T(4,128)S(1)} %slice.7), channel_id=1, source_target_pairs={{0,16},{16,32},{32,48},{48,64},{64,80},{80,96},{96,112},{1,17},{17... | collective-permute-start | bytes 6152 | tf_op jit(solution)/shard_map/ppermute | solution.py:33
  56.2 2.4 %collective-permute-done.1 = f32[4,128]{1,0:T(4,128)S(1)} collective-permute-done((f32[4,128]{1,0:T(4,128)S(1)}, f32[4,128]{1,0:T(4,128)S(1)}, u32[]{:S(2)}, u32[]{:S(2)}) %collective-permute-start.1) | collective-permute-done | bytes 2080 | tf_op jit(solution)/shard_map/ppermute | solution.py:33
  58.6 0.6 add_bitcast_fusion
  (2 shorter events, 0.0 us)
Async XLA Ops:
  17.9 15.3 %collective-permute-start = (f32[16,56,128]{2,1,0:T(8,128)S(1)}, f32[16,56,128]{2,1,0:T(8,128)S(1)}, u32[]{:S(2)}, u32[]{:S(2)}) collective-permute-start(f32[16,56,128]{2,1,0:T(8,128)S(1)} %all_to_all.10.received), channel_id=1, source_target_pairs={{16,0},{32,16},{48,32},{64,48},{80,64},{96,80},{112,96},{17,1},{33... | collective-permute-start | bytes 1376264 | tf_op jit(solution)/shard_map/ppermute | solution.py:33
  50.7 7.9 %collective-permute-start.1 = (f32[4,128]{1,0:T(4,128)S(1)}, f32[4,128]{1,0:T(4,128)S(1)}, u32[]{:S(2)}, u32[]{:S(2)}) collective-permute-start(f32[4,128]{1,0:T(4,128)S(1)} %slice.7), channel_id=1, source_target_pairs={{0,16},{16,32},{32,48},{48,64},{64,80},{80,96},{96,112},{1,17},{17... | collective-permute-start | bytes 6152 | tf_op jit(solution)/shard_map/ppermute | solution.py:33
